TPU v7x, 256 devices: a whole 4x4x8 slice. The times are simulated.
256 devices in a mesh: band: 8 (over x, core), dom: 32 (over z, y).
Axes of the slice: x: 4, y: 4, z: 8, core: 2. Of those that a mesh axis runs over, the one named last changes fastest.
Arguments:
- orbitals: float32 [64, 256, 16, 128], P('band', 'dom'), may hold values from -16 to 16
- potential: float32 [256, 16, 128], P('dom'), may hold values from -10 to 2
Outputs:
- filtered: float32 [64, 256, 16, 128], P('band', 'dom')
- hamiltonian: float32 [64, 64], P('band')
- margin: float32 [64, 64], P('band')
All inputs are finite; a program needn't handle non-finite values.
Results may differ from a plain program's by a relative error of at most 0.000077.
Values sent between devices are 32-bit elements; how exact they have to be, the bound alone decides.
A program may use at most 128 MiB of HBM per device.

v0:
```python
import jax
import jax.numpy as jnp
import ml_dtypes
import numpy as np
from jax import lax
from jax.experimental import pallas as pl
from jax.experimental.pallas import tpu as pltpu
from jax.sharding import PartitionSpec as P

MESH = pl.DeviceIdType.MESH

stencil_weights = (
    -5369.0 / 1800.0,
    12.0 / 7.0,
    -15.0 / 56.0,
    10.0 / 189.0,
    -1.0 / 112.0,
    2.0 / 825.0,
    -1.0 / 2772.0,
)
spacing = 0.35
kinetic = -0.5 / (spacing * spacing)
upper_bound = 90.0
cutoff = 8.0
lower_bound = -11.0
center = (upper_bound + cutoff) / 2.0
half_width = (upper_bound - cutoff) / 2.0
first_ratio = half_width / (lower_bound - center)
second_ratio = 1.0 / (2.0 / first_ratio - first_ratio)
first_scale = first_ratio / half_width
second_scale = 2.0 * second_ratio / half_width

NB = 8
NY = 4
NZ = 8
ORB = 8
NS = ORB // NY
LAYERS = 8
CHUNK = NY * LAYERS
REACH = 6
PLANE = NB * NY - 1
TOTAL = 256 * 16 * 128
bf16 = jnp.bfloat16
f32 = jnp.float32


def in_plane_matrices(both_sides):
    def circulant(n):
        shift = (np.arange(n)[:, None] - np.arange(n)[None, :]) % n
        matrix = np.zeros((n, n))
        for o in range(1, REACH + 1):
            matrix += stencil_weights[o] * (shift == o)
            if both_sides:
                matrix += stencil_weights[o] * (shift == n - o)
        return matrix

    def parts(matrix):
        matrix = matrix.astype(np.float32)
        high = matrix.astype(ml_dtypes.bfloat16)
        return high, (matrix - high.astype(np.float32)).astype(ml_dtypes.bfloat16)

    y_high, y_low = parts(circulant(128))
    x_high, x_low = parts(np.kron(np.eye(8), circulant(16)))
    along_y = np.block([[y_high, y_low], [y_high, np.zeros_like(y_low)]])
    return along_y, np.concatenate([x_high, x_high, x_low], axis=1)


def split(value):
    high = value.astype(bf16)
    return high, (value - high.astype(f32)).astype(bf16)


def in_plane(mid, along_y, along_x):
    high, low = split(mid.reshape(8 * 16, 128))
    y_sum = jnp.dot(jnp.concatenate([high, low], axis=1), along_y[...], preferred_element_type=f32)
    x_sum = jnp.dot(
        along_x[...], jnp.concatenate([high, low, high], axis=0), preferred_element_type=f32
    )
    return (y_sum[:, :128] + y_sum[:, 128:] + x_sum).reshape(8, 16, 128)


def full_stencil(src, first, potential, scale, along_y, along_x):
    layer = [src[first + z] for z in range(8 + 2 * REACH)]
    mid = jnp.stack(layer[REACH : REACH + 8])
    normal = []
    for z in range(REACH, REACH + 8):
        total = stencil_weights[1] * (layer[z + 1] + layer[z - 1])
        for o in range(2, REACH + 1):
            total = total + stencil_weights[o] * (layer[z + o] + layer[z - o])
        normal.append(total)
    sums = jnp.stack(normal) + in_plane(mid, along_y, along_x)
    diagonal = scale * (potential + (3.0 * kinetic * stencil_weights[0] - center))
    return (scale * kinetic) * sums + diagonal * mid


def half_stencil(src, first, potential, along_y, along_x):
    mid = src[pl.ds(first + REACH, 8)]
    above = [src[first + REACH + z, 0:8] for z in range(8 + REACH)]
    below = [src[first + z, 8:16] for z in range(8 + REACH)]
    normal = []
    for z in range(8):
        up = stencil_weights[1] * above[z + 1]
        down = stencil_weights[1] * below[z + REACH - 1]
        for o in range(2, REACH + 1):
            up = up + stencil_weights[o] * above[z + o]
            down = down + stencil_weights[o] * below[z + REACH - o]
        normal.append(jnp.concatenate([up, down], axis=0))
    sums = jnp.stack(normal) + in_plane(mid, along_y, along_x)
    return kinetic * sums + (0.5 * potential + 1.5 * kinetic * stencil_weights[0]) * mid


def kernel(
    orb_hbm, pot_hbm, mats_hbm0, mats_hbm1, mats_hbm2, mats_hbm3, f_ref, rows_ref,
    full_y, full_x, half_y, half_x,
    o_home, v_share, v_buf, o_buf, u_buf, f_buf, g_buf, f_all, g_all, f_parts, y_rows,
    m_part, m_band, m_dom, h_part, h_band, h_dom,
    load_sem, in_send, in_recv, v_send, v_recv, z_send, z_recv, h_send, h_recv,
    f_send, f_recv, g_send, g_recv, out_send, out_recv, m_send, m_recv, r_send, r_recv, relay,
):
    band = lax.axis_index("band")
    dom = lax.axis_index("dom")
    y = lax.rem(dom, NY)
    z = lax.div(dom, NY)
    z_up = lax.rem(z + 1, NZ) * NY + y
    z_down = lax.rem(z + NZ - 1, NZ) * NY + y
    y_peers = [lax.rem(y + j, NY) for j in (1, 3, 2)]
    band_peers = [lax.rem(band + j, NB) for j in (4, 3, 5, 2, 6, 1, 7)]
    z_rows = [lax.rem(z + j, NZ) * NY for j in range(NZ)]
    y_columns = [lax.rem(y + j, NY) for j in range(NY)]
    offsets = [(i, j) for i in range(NZ) for j in range(NY) if i or j]
    offsets.sort(key=lambda ij: -min(ij[0], NZ - ij[0]) - min(ij[1], NY - ij[1]))
    dom_peers = [z_rows[i] + y_columns[j] for i, j in offsets]

    band_ring = [lax.rem(band + j, NB) for j in range(NB)]
    y_layers = [LAYERS * lax.rem(y + i, NY) for i in range(NY)]
    dom_ring = [z * NY + lax.rem(y + i, NY) for i in range(NY)]

    barrier = pltpu.get_barrier_semaphore()
    for peer in [z_up, z_down] + [z * NY + peer for peer in y_peers]:
        pl.semaphore_signal(barrier, inc=1, device_id={"dom": peer}, device_id_type=MESH)
    for peer in band_peers:
        pl.semaphore_signal(barrier, inc=1, device_id={"band": peer}, device_id_type=MESH)

    loads = [
        pltpu.make_async_copy(orb_hbm, o_home, load_sem.at[0]),
        pltpu.make_async_copy(pot_hbm.at[band], v_share.at[band, y], load_sem.at[1]),
        pltpu.make_async_copy(mats_hbm0, full_y, load_sem.at[2]),
        pltpu.make_async_copy(mats_hbm1, full_x, load_sem.at[3]),
        pltpu.make_async_copy(mats_hbm2, half_y, load_sem.at[4]),
        pltpu.make_async_copy(mats_hbm3, half_x, load_sem.at[5]),
        pltpu.make_async_copy(
            orb_hbm.at[pl.ds(NS * y, NS)],
            o_buf.at[:, pl.ds(2 * REACH + LAYERS * y, LAYERS)],
            load_sem.at[6],
        ),
    ]
    for load in loads:
        load.start()
    for load in loads:
        load.wait()
    pl.semaphore_wait(barrier, 2 + (NY - 1) + (NB - 1))

    def remote(src, dst, send, recv, where):
        return pltpu.make_async_remote_copy(
            src_ref=src, dst_ref=dst, send_sem=send, recv_sem=recv,
            device_id=where, device_id_type=MESH,
        )

    def wait_bytes(ref, sem):
        pltpu.make_async_copy(ref, ref, sem).wait()

    def in_copy(s, peer):
        return remote(
            o_home.at[NS * peer + s], o_buf.at[s, pl.ds(2 * REACH + LAYERS * y, LAYERS)],
            in_send.at[s], in_recv.at[s], {"dom": z * NY + peer},
        )

    def z_copies(src, width, send, recv):
        low, high = src.shape[0] - width, src.shape[0] - 2 * width
        return (
            remote(src.at[high:low], src.at[0:width], send.at[0], recv.at[0], {"dom": z_up}),
            remote(src.at[width : 2 * width], src.at[low:], send.at[1], recv.at[1], {"dom": z_down}),
        )

    def o_halo(s):
        return z_copies(o_buf.at[s], 2 * REACH, z_send.at[s], z_recv.at[s])

    def f_halo(s):
        src = f_buf.at[s]
        return (
            remote(
                src.at[CHUNK : CHUNK + REACH, 8:16], src.at[0:REACH, 8:16],
                h_send.at[s, 0], h_recv.at[s, 0], {"dom": z_up},
            ),
            remote(
                src.at[REACH : 2 * REACH, 0:8], src.at[CHUNK + REACH :, 0:8],
                h_send.at[s, 1], h_recv.at[s, 1], {"dom": z_down},
            ),
        )

    def v_round(slots, i):
        for peer in band_peers:
            src = v_share.at[band, slots]
            remote(src, src, v_send.at[i], v_recv.at[i], {"band": peer}).start()

    for peer in y_peers:
        src = v_share.at[band, y]
        remote(src, src, v_send.at[0], v_recv.at[0], {"dom": z * NY + peer}).start()
    for peer in y_peers:
        in_copy(0, peer).start()
    wait_bytes(v_share.at[0, 0 : NY - 1], v_recv.at[0])
    for peer in y_peers:
        in_copy(1, peer).start()
    remote(
        v_share.at[band, NY - 1], v_share.at[band, NY], v_send.at[1], v_recv.at[1], {"dom": z_up}
    ).start()
    remote(
        v_share.at[band, 0], v_share.at[band, NY + 1], v_send.at[1], v_recv.at[1], {"dom": z_down}
    ).start()
    v_round(slice(0, NY), 2)
    wait_bytes(o_home.at[0 : NY - 1], in_recv.at[0])
    for copy in o_halo(0):
        copy.start()
    wait_bytes(v_share.at[0, 0:2], v_recv.at[1])
    v_round(slice(NY, NY + 2), 3)
    wait_bytes(v_share.at[0 : NB - 1, 0:NY], v_recv.at[2])
    for layer in range(CHUNK):
        v_buf[REACH + layer] = v_share[layer % NB, layer // NB]
    wait_bytes(o_home.at[0 : NY - 1], in_recv.at[1])
    for copy in o_halo(1):
        copy.start()

    def first_term(s, firsts):
        for first in firsts:
            u_buf[s, first : first + 8] = full_stencil(
                o_buf.at[s], first, v_buf[first : first + 8], first_scale, full_y, full_x
            )

    for s in range(NS):
        first_term(s, (12, 20))
    wait_bytes(v_share.at[0 : NB - 1, 0:2], v_recv.at[3])
    for layer in range(REACH):
        v_buf[layer] = v_share[NB - REACH + layer, NY]
        v_buf[REACH + CHUNK + layer] = v_share[layer, NY + 1]

    def share(src, dst, s, send, recv):
        for n in range(1, PLANE + 1):
            j, i = 13 * n % (PLANE + 1) % NB, 13 * n % (PLANE + 1) // NB
            remote(
                src.at[y_layers[i] + band_ring[j]], dst.at[ORB * band + NS * y + s],
                send.at[s], recv.at[s], {"band": band_ring[j], "dom": dom_ring[i]},
            ).start()

        dst[ORB * band + NS * y + s] = src[LAYERS * y + band]

    @pl.loop(0, NS)
    def _(s):
        for copy in o_halo(s):
            copy.wait_recv()
        first_term(s, (0, 4, 28, 36))
        for first in range(0, CHUNK, 8):
            value = full_stencil(
                u_buf.at[s], first, v_buf[REACH + first : REACH + first + 8], second_scale, full_y, full_x
            )
            old = o_buf[s, 2 * REACH + first : 2 * REACH + first + 8]
            f_buf[s, REACH + first : REACH + first + 8] = value - (first_ratio * second_ratio) * old
        for copy in f_halo(s):
            copy.start()
        share(f_buf.at[s, REACH : REACH + CHUNK], f_all, s, f_send, f_recv)

    @pl.loop(0, NS)
    def _(s):
        for copy in f_halo(s):
            copy.wait_recv()
        for first in range(0, CHUNK, 8):
            g_buf[s, first : first + 8] = half_stencil(
                f_buf.at[s], first, v_buf[REACH + first : REACH + first + 8], half_y, half_x
            )
        share(g_buf.at[s], g_all, s, g_send, g_recv)

    for i in range(2):
        pl.semaphore_signal(relay.at[i, 0], inc=1, device_id={"dom": z_up}, device_id_type=MESH)
        pl.semaphore_signal(relay.at[i, 1], inc=1, device_id={"dom": z_down}, device_id_type=MESH)
        for j in range(2):
            pl.semaphore_wait(relay.at[i, j], 1)

    def out_copy(s, peer):
        return remote(
            f_buf.at[s, pl.ds(REACH + LAYERS * peer, LAYERS)], f_ref.at[NS * y + s],
            out_send, out_recv, {"dom": z * NY + peer},
        )

    for s in range(NS):
        for peer in y_peers:
            out_copy(s, peer).start()
        f_ref[NS * y + s] = f_buf[s, pl.ds(REACH + LAYERS * y, LAYERS)]

    def pieces(rows, first, count, stride, c):
        value = jnp.concatenate(
            [rows[pl.ds(first + 2 * c + i, count, stride=stride), :] for i in range(2)], axis=1
        )
        return jnp.concatenate(split(value), axis=0)

    def against_f(left, c):
        return lax.dot_general(
            left, f_parts[c], (((1,), (1,)), ((), ())), preferred_element_type=f32
        )

    f_rows = f_all.reshape(NB * ORB * 16, 128)
    g_rows = g_all.reshape(NB * ORB * 16, 128)
    for s in range(NS):
        wait_bytes(f_all.at[0:PLANE], f_recv.at[s])
    total = jnp.zeros((128, 128), f32)
    for c in range(8):
        left = pieces(f_rows, 0, 64, 16, c)
        f_parts[c] = left
        total = total + against_f(left, c)
    lane = lax.broadcasted_iota(jnp.int32, (NB, 4, 128), 2)

    def band_tiles(value):
        value = value.reshape(NB, 8, 128)
        return jnp.where(lane < 64, value[:, 0:4], value[:, 4:8])

    def total_of(slots, count):
        total = slots[0]
        for i in range(1, count):
            total = total + slots[i]
        return total

    def over_band(tiles, slots, send, recv):
        for peer in band_peers:
            remote(tiles.at[peer], slots.at[band], send.at[0], recv.at[0], {"band": peer}).start()
        slots[band] = tiles[band]

    def over_dom(tiles, slots, send, recv):
        wait_bytes(tiles.at[0 : NB - 1], recv.at[0])
        slots[dom] = total_of(tiles, NB)
        for peer in dom_peers:
            remote(slots.at[dom], slots.at[dom], send.at[1], recv.at[1], {"dom": peer}).start()

    def result(slots, recv):
        wait_bytes(slots.at[0 : NY * NZ - 1], recv.at[1])
        return total_of(slots, NY * NZ) * (1.0 / TOTAL)

    margin = total[0:64] + total[64:128]
    m_part[...] = band_tiles(margin + pltpu.roll(margin, 64, 1))
    over_band(m_part, m_band, m_send, m_recv)
    for s in range(NS):
        wait_bytes(g_all.at[0:PLANE], g_recv.at[s])
        total = jnp.zeros((64, 128), f32)
        for c in range(8):
            total = total + against_f(pieces(g_rows, 16 * s, 32, 32, c), c)
        total = total[0:32] + total[32:64]
        y_rows[pl.ds(s, 32, stride=2), :] = total + pltpu.roll(total, 64, 1)
        if s == 0:
            over_dom(m_band, m_dom, m_send, m_recv)
    one_side = y_rows[...]
    other_side = jnp.concatenate([one_side, one_side], axis=0).T
    h_part[...] = band_tiles(one_side + other_side[0:64])
    over_band(h_part, h_band, r_send, r_recv)
    over_dom(h_band, h_dom, r_send, r_recv)
    margin = result(m_dom, m_recv)
    hamil = result(h_dom, r_recv)
    margin = jnp.concatenate([margin, pltpu.roll(margin, 64, 1)], axis=0)
    hamil = jnp.concatenate([pltpu.roll(hamil, 64, 1), hamil], axis=0)
    rows_ref[...] = jnp.where(lax.broadcasted_iota(jnp.int32, (8, 128), 1) < 64, margin, hamil)

    wait_bytes(o_home.at[0 : NS * (NY - 1)], out_recv)
    wait_bytes(o_home.at[0 : NS * (NY - 1)], out_send)
    wait_bytes(v_share.at[0, 0 : NY - 1], v_send.at[0])
    wait_bytes(v_share.at[0, 0:2], v_send.at[1])
    wait_bytes(v_share.at[0 : NB - 1, 0:NY], v_send.at[2])
    wait_bytes(v_share.at[0 : NB - 1, 0:2], v_send.at[3])

    @pl.loop(0, NS)
    def _(s):
        wait_bytes(o_home.at[0 : NY - 1], in_send.at[s])
        for copy in o_halo(s) + f_halo(s):
            copy.wait_send()
        wait_bytes(f_all.at[0:PLANE], f_send.at[s])
        wait_bytes(g_all.at[0:PLANE], g_send.at[s])

    for send in (m_send, r_send):
        wait_bytes(h_dom.at[0 : NB - 1], send.at[0])
        wait_bytes(h_dom.at[0 : NY * NZ - 1], send.at[1])


def finish(f_ref, rows_ref, out_hbm, ham_hbm, mar_hbm, ham, mar, sems):
    copies = [
        pltpu.make_async_copy(f_ref.at[2 * i : 2 * i + 2], out_hbm.at[2 * i : 2 * i + 2], sems.at[i])
        for i in range(4)
    ]
    copies.append(pltpu.make_async_copy(ham, ham_hbm, sems.at[4]))
    copies.append(pltpu.make_async_copy(mar, mar_hbm, sems.at[5]))
    for copy in copies[:4]:
        copy.start()
    ham[...] = rows_ref[:, 64:128]
    mar[...] = rows_ref[:, 0:64]
    for copy in copies[4:]:
        copy.start()
    for copy in copies:
        copy.wait()


def on_device(orbitals, potential):
    dma = pltpu.SemaphoreType.DMA
    in_hbm = pl.BlockSpec(memory_space=pltpu.HBM)
    in_vmem = pl.BlockSpec(memory_space=pltpu.VMEM)
    matrices = [jnp.asarray(m) for both in (True, False) for m in in_plane_matrices(both)]
    filtered, rows = pl.pallas_call(
        kernel,
        out_shape=(
            pltpu.VMEM((ORB, LAYERS, 16, 128), f32),
            pltpu.VMEM((8, 128), f32),
        ),
        in_specs=[in_hbm] * 6,
        out_specs=(in_vmem, in_vmem),
        scratch_shapes=[
            pltpu.VMEM((256, 256), bf16),
            pltpu.VMEM((128, 384), bf16),
            pltpu.VMEM((256, 256), bf16),
            pltpu.VMEM((128, 384), bf16),
            pltpu.VMEM((ORB, LAYERS, 16, 128), f32),
            pltpu.VMEM((NB, NY + 2, 16, 128), f32),
            pltpu.VMEM((CHUNK + 2 * REACH, 16, 128), f32),
            pltpu.VMEM((NS, CHUNK + 4 * REACH, 16, 128), f32),
            pltpu.VMEM((NS, CHUNK + 2 * REACH, 16, 128), f32),
            pltpu.VMEM((NS, CHUNK + 2 * REACH, 16, 128), f32),
            pltpu.VMEM((NS, CHUNK, 16, 128), f32),
            pltpu.VMEM((NB * ORB, 16, 128), f32),
            pltpu.VMEM((NB * ORB, 16, 128), f32),
            pltpu.VMEM((8, 128, 256), bf16),
            pltpu.VMEM((64, 128), f32),
            pltpu.VMEM((NB, 4, 128), f32),
            pltpu.VMEM((NB, 4, 128), f32),
            pltpu.VMEM((NY * NZ, 4, 128), f32),
            pltpu.VMEM((NB, 4, 128), f32),
            pltpu.VMEM((NB, 4, 128), f32),
            pltpu.VMEM((NY * NZ, 4, 128), f32),
            dma((7,)),
            dma((NS,)), dma((NS,)),
            dma((4,)), dma((4,)),
            dma((NS, 2)), dma((NS, 2)),
            dma((NS, 2)), dma((NS, 2)),
            dma((NS,)), dma((NS,)), dma((NS,)), dma((NS,)),
            dma, dma, dma((2,)), dma((2,)), dma((2,)), dma((2,)),
            pltpu.SemaphoreType.REGULAR((2, 2)),
        ],
        compiler_params=pltpu.CompilerParams(
            collective_id=0, has_side_effects=True, vmem_limit_bytes=60 * 1024 * 1024
        ),
    )(orbitals, potential, *matrices)
    return pl.pallas_call(
        finish,
        out_shape=(
            jax.ShapeDtypeStruct((ORB, LAYERS, 16, 128), f32),
            jax.ShapeDtypeStruct((8, 64), f32),
            jax.ShapeDtypeStruct((8, 64), f32),
        ),
        in_specs=[in_vmem, in_vmem],
        out_specs=(in_hbm, in_hbm, in_hbm),
        scratch_shapes=[pltpu.VMEM((8, 64), f32), pltpu.VMEM((8, 64), f32), dma((6,))],
        compiler_params=pltpu.CompilerParams(vmem_limit_bytes=16 * 1024 * 1024),
    )(filtered, rows)


def solution(mesh):
    in_specs = (P("band", "dom", None, None), P("dom", None, None))
    out_specs = (P("band", "dom", None, None), P("band", None), P("band", None))
    return jax.shard_map(
        on_device, mesh=mesh, in_specs=in_specs, out_specs=out_specs, check_vma=False
    )
```

profile of v0, /device:TPU:1, one launch (start us, length us, event | category | flops | bytes accessed | tf_op | source)
XLA Modules:
  0.0 46.6 jit_solution(12129476706192192313)
XLA Ops:
  0.6 45.2 %shard_map.85 = (f32[8,8,16,128]{3,2,1,0:T(8,128)S(1)}, f32[8,128]{1,0:T(8,128)S(1)}) custom-call(f32[8,8,16,128]{3,2,1,0:T(8,128)} %orb_hbm.1, f32[8,16,128]{2,1,0:T(8,128)} %pot_hbm.1, bf16[256,256]{1,0:T(8,128)(2,1)} %constant.8.clone.mats_hbm0, bf16[128,384]{1,0:T(8,128)(2,1)} %constant.9.clone.mats_hbm1, bf16[256,256]{1,0:T(8,128)(2,1)} %constant.10.clone.mats_hbm2, ...), custom_call_target="tpu_custom_call" | custom-call | tf_op jit(solution)/shard_map/pallas_call | solution.py:410
  45.8 0.8 %shard_map.86 = (f32[8,8,16,128]{3,2,1,0:T(8,128)}, f32[8,64]{1,0:T(8,128)}, f32[8,64]{1,0:T(8,128)}) custom-call(f32[8,8,16,128]{3,2,1,0:T(8,128)S(1)} %get-tuple-element.5.f_ref, f32[8,128]{1,0:T(8,128)S(1)} %get-tuple-element.6.rows_ref), custom_call_target="tpu_custom_call" | custom-call | tf_op jit(solution)/shard_map/pallas_call | solution.py:453
where the time goes:
time: 46.7 us; the launch traced here: 46.6 us
  Pallas kernels  46 us (99%)
  between operations  0.64 us (1%)
    pallas_call x1, Pallas kernels, on_device(): pl.pallas_call(kernel, out_shape=(pltpu.VMEM((ORB, LAYERS, 16, 128), f32)...  45.2 us

commit v1 on v0

--- a/solution.py
+++ b/solution.py
@@ -125,15 +125,6 @@
     z_down = lax.rem(z + NZ - 1, NZ) * NY + y
     y_peers = [lax.rem(y + j, NY) for j in (1, 3, 2)]
     band_peers = [lax.rem(band + j, NB) for j in (4, 3, 5, 2, 6, 1, 7)]
-    z_rows = [lax.rem(z + j, NZ) * NY for j in range(NZ)]
-    y_columns = [lax.rem(y + j, NY) for j in range(NY)]
-    offsets = [(i, j) for i in range(NZ) for j in range(NY) if i or j]
-    offsets.sort(key=lambda ij: -min(ij[0], NZ - ij[0]) - min(ij[1], NY - ij[1]))
-    dom_peers = [z_rows[i] + y_columns[j] for i, j in offsets]
-
-    band_ring = [lax.rem(band + j, NB) for j in range(NB)]
-    y_layers = [LAYERS * lax.rem(y + i, NY) for i in range(NY)]
-    dom_ring = [z * NY + lax.rem(y + i, NY) for i in range(NY)]
 
     barrier = pltpu.get_barrier_semaphore()
     for peer in [z_up, z_down] + [z * NY + peer for peer in y_peers]:
@@ -156,6 +147,16 @@
     ]
     for load in loads:
         load.start()
+    z_rows = [lax.rem(z + j, NZ) * NY for j in range(NZ)]
+    y_columns = [lax.rem(y + j, NY) for j in range(NY)]
+    offsets = [(i, j) for i in range(NZ) for j in range(NY) if i or j]
+    offsets.sort(key=lambda ij: -min(ij[0], NZ - ij[0]) - min(ij[1], NY - ij[1]))
+    dom_peers = [z_rows[i] + y_columns[j] for i, j in offsets]
+
+    band_ring = [lax.rem(band + j, NB) for j in range(NB)]
+    y_layers = [LAYERS * lax.rem(y + i, NY) for i in range(NY)]
+    dom_ring = [z * NY + lax.rem(y + i, NY) for i in range(NY)]
+
     for load in loads:
         load.wait()
     pl.semaphore_wait(barrier, 2 + (NY - 1) + (NB - 1))
@@ -197,6 +198,14 @@
                 h_send.at[s, 1], h_recv.at[s, 1], {"dom": z_down},
             ),
         )
+
+    def pass_on(i):
+        pl.semaphore_signal(relay.at[i, 0], inc=1, device_id={"dom": z_up}, device_id_type=MESH)
+        pl.semaphore_signal(relay.at[i, 1], inc=1, device_id={"dom": z_down}, device_id_type=MESH)
+
+    def hear(i):
+        for j in range(2):
+            pl.semaphore_wait(relay.at[i, j], 1)
 
     def v_round(slots, i):
         for peer in band_peers:
@@ -223,6 +232,7 @@
         copy.start()
     wait_bytes(v_share.at[0, 0:2], v_recv.at[1])
     v_round(slice(NY, NY + 2), 3)
+    pass_on(0)
     wait_bytes(v_share.at[0 : NB - 1, 0:NY], v_recv.at[2])
     for layer in range(CHUNK):
         v_buf[REACH + layer] = v_share[layer % NB, layer // NB]
@@ -243,46 +253,51 @@
         v_buf[layer] = v_share[NB - REACH + layer, NY]
         v_buf[REACH + CHUNK + layer] = v_share[layer, NY + 1]
 
-    def share(src, dst, s, send, recv):
-        for n in range(1, PLANE + 1):
-            j, i = 13 * n % (PLANE + 1) % NB, 13 * n % (PLANE + 1) // NB
-            remote(
-                src.at[y_layers[i] + band_ring[j]], dst.at[ORB * band + NS * y + s],
-                send.at[s], recv.at[s], {"band": band_ring[j], "dom": dom_ring[i]},
-            ).start()
-
-        dst[ORB * band + NS * y + s] = src[LAYERS * y + band]
+    def share_layers(i, src, dst, s, send, recv):
+        slot = ORB * band + NS * y + s
+        for j in (3, 6, 1, 4, 7, 2, 5, 0):
+            if i or j:
+                remote(
+                    src.at[y_layers[i] + band_ring[j]], dst.at[slot],
+                    send.at[s], recv.at[s], {"band": band_ring[j], "dom": dom_ring[i]},
+                ).start()
+        if i == 0:
+            dst[slot] = src[LAYERS * y + band]
+
+    hear(0)
+    pass_on(1)
 
     @pl.loop(0, NS)
     def _(s):
         for copy in o_halo(s):
             copy.wait_recv()
         first_term(s, (0, 4, 28, 36))
-        for first in range(0, CHUNK, 8):
+        for i in (1, 3, 2, 0):
+            first = y_layers[i]
             value = full_stencil(
-                u_buf.at[s], first, v_buf[REACH + first : REACH + first + 8], second_scale, full_y, full_x
+                u_buf.at[s], first, v_buf[pl.ds(REACH + first, 8)], second_scale, full_y, full_x
             )
-            old = o_buf[s, 2 * REACH + first : 2 * REACH + first + 8]
-            f_buf[s, REACH + first : REACH + first + 8] = value - (first_ratio * second_ratio) * old
+            old = o_buf[s, pl.ds(2 * REACH + first, 8)]
+            f_buf[s, pl.ds(REACH + first, 8)] = value - (first_ratio * second_ratio) * old
+            share_layers(i, f_buf.at[s, REACH : REACH + CHUNK], f_all, s, f_send, f_recv)
         for copy in f_halo(s):
             copy.start()
-        share(f_buf.at[s, REACH : REACH + CHUNK], f_all, s, f_send, f_recv)
+
+    hear(1)
+    pass_on(2)
 
     @pl.loop(0, NS)
     def _(s):
         for copy in f_halo(s):
             copy.wait_recv()
-        for first in range(0, CHUNK, 8):
-            g_buf[s, first : first + 8] = half_stencil(
-                f_buf.at[s], first, v_buf[REACH + first : REACH + first + 8], half_y, half_x
+        for i in (1, 3, 2, 0):
+            first = y_layers[i]
+            g_buf[s, pl.ds(first, 8)] = half_stencil(
+                f_buf.at[s], first, v_buf[pl.ds(REACH + first, 8)], half_y, half_x
             )
-        share(g_buf.at[s], g_all, s, g_send, g_recv)
-
-    for i in range(2):
-        pl.semaphore_signal(relay.at[i, 0], inc=1, device_id={"dom": z_up}, device_id_type=MESH)
-        pl.semaphore_signal(relay.at[i, 1], inc=1, device_id={"dom": z_down}, device_id_type=MESH)
-        for j in range(2):
-            pl.semaphore_wait(relay.at[i, j], 1)
+            share_layers(i, g_buf.at[s], g_all, s, g_send, g_recv)
+
+    hear(2)
 
     def out_copy(s, peer):
         return remote(
@@ -444,7 +459,7 @@
             dma((NS, 2)), dma((NS, 2)),
             dma((NS,)), dma((NS,)), dma((NS,)), dma((NS,)),
             dma, dma, dma((2,)), dma((2,)), dma((2,)), dma((2,)),
-            pltpu.SemaphoreType.REGULAR((2, 2)),
+            pltpu.SemaphoreType.REGULAR((3, 2)),
         ],
         compiler_params=pltpu.CompilerParams(
             collective_id=0, has_side_effects=True, vmem_limit_bytes=60 * 1024 * 1024

time: 46.7 us -> 46.7 us (level)
  no operation moved by 1% of the time
where the time goes in v1:
time: 46.7 us; the launch traced here: 46.6 us
  Pallas kernels  45.9 us (98%)
  between operations  0.64 us (1%)
    pallas_call x1, Pallas kernels, on_device(): pl.pallas_call(kernel, out_shape=(pltpu.VMEM((ORB, LAYERS, 16, 128), f32)...  45.1 us

profile of v1, /device:TPU:1, one launch (start us, length us, event | category | flops | bytes accessed | tf_op | source)
XLA Modules:
  0.0 46.6 jit_solution(13254641678264498956)
XLA Ops:
  0.6 45.1 %shard_map.85 = (f32[8,8,16,128]{3,2,1,0:T(8,128)S(1)}, f32[8,128]{1,0:T(8,128)S(1)}) custom-call(f32[8,8,16,128]{3,2,1,0:T(8,128)} %orb_hbm.1, f32[8,16,128]{2,1,0:T(8,128)} %pot_hbm.1, bf16[256,256]{1,0:T(8,128)(2,1)} %constant.8.clone.mats_hbm0, bf16[128,384]{1,0:T(8,128)(2,1)} %constant.9.clone.mats_hbm1, bf16[256,256]{1,0:T(8,128)(2,1)} %constant.10.clone.mats_hbm2, ...), custom_call_target="tpu_custom_call" | custom-call | tf_op jit(solution)/shard_map/pallas_call | solution.py:425
  45.7 0.8 %shard_map.86 = (f32[8,8,16,128]{3,2,1,0:T(8,128)}, f32[8,64]{1,0:T(8,128)}, f32[8,64]{1,0:T(8,128)}) custom-call(f32[8,8,16,128]{3,2,1,0:T(8,128)S(1)} %get-tuple-element.5.f_ref, f32[8,128]{1,0:T(8,128)S(1)} %get-tuple-element.6.rows_ref), custom_call_target="tpu_custom_call" | custom-call | tf_op jit(solution)/shard_map/pallas_call | solution.py:468

commit v2 on v1

--- a/solution.py
+++ b/solution.py
@@ -321,8 +321,8 @@
             left, f_parts[c], (((1,), (1,)), ((), ())), preferred_element_type=f32
         )
 
-    f_rows = f_all.reshape(NB * ORB * 16, 128)
-    g_rows = g_all.reshape(NB * ORB * 16, 128)
+    f_rows = f_all.reshape((NB * ORB + 2) * 16, 128)
+    g_rows = g_all.reshape((NB * ORB + 2) * 16, 128)
     for s in range(NS):
         wait_bytes(f_all.at[0:PLANE], f_recv.at[s])
     total = jnp.zeros((128, 128), f32)
@@ -369,7 +369,7 @@
         y_rows[pl.ds(s, 32, stride=2), :] = total + pltpu.roll(total, 64, 1)
         if s == 0:
             over_dom(m_band, m_dom, m_send, m_recv)
-    one_side = y_rows[...]
+    one_side = y_rows[0:64]
     other_side = jnp.concatenate([one_side, one_side], axis=0).T
     h_part[...] = band_tiles(one_side + other_side[0:64])
     over_band(h_part, h_band, r_send, r_recv)
@@ -442,10 +442,10 @@
             pltpu.VMEM((NS, CHUNK + 2 * REACH, 16, 128), f32),
             pltpu.VMEM((NS, CHUNK + 2 * REACH, 16, 128), f32),
             pltpu.VMEM((NS, CHUNK, 16, 128), f32),
-            pltpu.VMEM((NB * ORB, 16, 128), f32),
-            pltpu.VMEM((NB * ORB, 16, 128), f32),
+            pltpu.VMEM((NB * ORB + 2, 16, 128), f32),
+            pltpu.VMEM((NB * ORB + 2, 16, 128), f32),
             pltpu.VMEM((8, 128, 256), bf16),
-            pltpu.VMEM((64, 128), f32),
+            pltpu.VMEM((72, 128), f32),
             pltpu.VMEM((NB, 4, 128), f32),
             pltpu.VMEM((NB, 4, 128), f32),
             pltpu.VMEM((NY * NZ, 4, 128), f32),

time: 46.7 us -> 46.7 us (level)
  no operation moved by 1% of the time
where the time goes in v2:
time: 46.7 us; the launch traced here: 46.6 us
  Pallas kernels  45.9 us (98%)
  between operations  0.64 us (1%)
    pallas_call x1, Pallas kernels, on_device(): pl.pallas_call(kernel, out_shape=(pltpu.VMEM((ORB, LAYERS, 16, 128), f32)...  45.1 us

profile of v2, /device:TPU:1, one launch (start us, length us, event | category | flops | bytes accessed | tf_op | source)
XLA Modules:
  0.0 46.6 jit_solution(17590161170324931625)
XLA Ops:
  0.6 45.1 %shard_map.85 = (f32[8,8,16,128]{3,2,1,0:T(8,128)S(1)}, f32[8,128]{1,0:T(8,128)S(1)}) custom-call(f32[8,8,16,128]{3,2,1,0:T(8,128)} %orb_hbm.1, f32[8,16,128]{2,1,0:T(8,128)} %pot_hbm.1, bf16[256,256]{1,0:T(8,128)(2,1)} %constant.8.clone.mats_hbm0, bf16[128,384]{1,0:T(8,128)(2,1)} %constant.9.clone.mats_hbm1, bf16[256,256]{1,0:T(8,128)(2,1)} %constant.10.clone.mats_hbm2, ...), custom_call_target="tpu_custom_call" | custom-call | tf_op jit(solution)/shard_map/pallas_call | solution.py:425
  45.7 0.8 %shard_map.86 = (f32[8,8,16,128]{3,2,1,0:T(8,128)}, f32[8,64]{1,0:T(8,128)}, f32[8,64]{1,0:T(8,128)}) custom-call(f32[8,8,16,128]{3,2,1,0:T(8,128)S(1)} %get-tuple-element.5.f_ref, f32[8,128]{1,0:T(8,128)S(1)} %get-tuple-element.6.rows_ref), custom_call_target="tpu_custom_call" | custom-call | tf_op jit(solution)/shard_map/pallas_call | solution.py:468
